TPU v7x, 256 devices: a whole 4x4x8 slice. The times are simulated.
256 devices in a mesh: tile: 32 (over z_lo, y, core), sample: 8 (over x, z_hi).
Axes of the slice: x: 4, y: 4, z: 8 (z_hi: 2, z_lo: 4; z = z_hi * 4 + z_lo), core: 2. Of those that a mesh axis runs over, the one named last changes fastest.
Arguments:
- inputs: bfloat16 [8, 16, 32, 1024], P('sample', None, 'tile'), may hold values from -6 to 6
- first_weight: bfloat16 [9, 1024, 1024], P(None, 'tile'), may hold values from -0.0625 to 0.0625
- second_weight: bfloat16 [9, 1024, 1024], P(None, 'tile'), may hold values from -0.0625 to 0.0625
- norm_gain_vector: float32 [1024], P('tile'), may hold values from 0.5 to 1.5
- norm_bias: float32 [1024], P('tile'), may hold values from -3 to 3
- cotangent: bfloat16 [8, 16, 32, 1024], P('sample', None, 'tile'), may hold values from -6 to 6
Outputs:
- input_grad: bfloat16 [8, 16, 32, 1024], P('sample', None, 'tile')
- first_grad: float32 [9, 1024, 1024], P(None, 'tile')
- second_grad: float32 [9, 1024, 1024], P(None, None, 'tile')
- gain_gradient: float32 [1024], P('tile')
- shift_grad: float32 [1024], P('tile')
All inputs are finite; a program needn't handle non-finite values.
Results may differ from a plain program's by a relative error of at most 0.0044.
Values may be sent and summed in bfloat16 or wider, within the bound.
No kernel may reach another device: no remote copies, remote signals or barrier semaphores. Data moves between devices by JAX's collectives and lax.ppermute only.
A program may use at most 64 MiB of HBM per device.

v0:
```python
import functools

import jax
import jax.numpy as jnp
from jax import lax
from jax.experimental import pallas as pl
from jax.experimental.pallas import tpu as pltpu
from jax.sharding import PartitionSpec as P

BF = jnp.bfloat16
F32 = jnp.float32
TAPS = [(dr, dc) for dr in (-1, 0, 1) for dc in (-1, 0, 1)]
ROWS, COLS, CH = 16, 32, 1024
POS = ROWS * COLS
OWN = 32
MB = 1 << 20

Z_MASKS, Y_MASKS, CORE = (8, 16, 24), (2, 4, 6), 1
ORDER = [c ^ y ^ z for c in (0, 1) for y in (0, 2, 4, 6) for z in (0, 8, 16, 24)]
SUM_ORDER = [c ^ y ^ z for c in (0, 1) for y in (0, 2, 4, 6) for z in (0, 8, 16, 24)]


def hop(value, mask, axis="tile", size=32):
    return lax.ppermute(value, axis, [(i, i ^ mask) for i in range(size)])


def shifted(value, dr, dc):
    step = ROWS * dc + dr
    moved = pltpu.roll(value, (-step) % POS, 1) if step else value
    if step == 0:
        return moved
    place = lax.broadcasted_iota(jnp.int32, value.shape, 1)
    row, col = place % ROWS + dr, place // ROWS + dc
    inside = (row >= 0) & (row < ROWS) & (col >= 0) & (col < COLS)
    return jnp.where(inside, moved, 0.0)


def assemble(me, near_ref, far_ref, out_ref, at):
    half = len(ORDER) // 2
    for k, mask in enumerate(ORDER):
        src = near_ref if k < half else far_ref
        out_ref[me ^ mask] = src[k % half, at : at + ROWS, :]


def x_index():
    return lax.axis_index("sample") // 2


def column(row):
    i = lax.broadcasted_iota(jnp.int32, (OWN, OWN), 0)
    j = lax.broadcasted_iota(jnp.int32, (OWN, OWN), 1)
    return jnp.sum(jnp.where(i == j, jnp.broadcast_to(row, (OWN, OWN)), 0.0), axis=1, keepdims=True)


def dot(a, b, ca, cb):
    return lax.dot_general(a, b, (((ca,), (cb,)), ((), ())), preferred_element_type=F32)


def forward_kernel(near_ref, far_ref, w1_ref, state_ref, x_ref):
    assemble(lax.axis_index("tile"), near_ref, far_ref, x_ref, 0)
    products = dot(w1_ref[...], x_ref[...].reshape(POS, CH), 1, 1)
    pre = jnp.zeros((OWN, POS), F32)
    for t, (dr, dc) in enumerate(TAPS):
        pre = pre + shifted(products[OWN * t : OWN * (t + 1)], dr, dc)
    count = 1.0 / (OWN * POS)
    mean = jnp.sum(pre, keepdims=True) * count
    centred = pre - mean
    rstd = lax.rsqrt(jnp.sum(centred * centred, keepdims=True) * count + 1e-05)
    state_ref[:OWN, :] = centred * rstd
    state_ref[OWN:, :] = jnp.broadcast_to(rstd, (8, POS))


def main_kernel(
    near_ref, far_ref, w2_ref, w1_ref, gain_ref, bias_ref, state_ref,
    p_near, p_far, g0, g1, g2, g3,
    x_ref, dy_ref, act_ref, w2t_ref, taps_ref, rows_ref, whole_ref,
):
    me = lax.axis_index("tile")
    assemble(me, near_ref, far_ref, x_ref, 0)
    xhat = state_ref[:OWN, :]
    rstd = state_ref[OWN : OWN + 1, 0:1]
    gain = column(gain_ref[...])
    normed = xhat * gain + column(bias_ref[...])
    sig = jax.nn.sigmoid(normed)
    act = (normed * sig).astype(BF).astype(F32)
    for t, (dr, dc) in enumerate(TAPS):
        act_ref[OWN * t : OWN * (t + 1), :] = shifted(act, dr, dc).astype(BF)
    slope = sig * (1.0 + normed * (1.0 - sig))
    assemble(me, near_ref, far_ref, dy_ref, ROWS)
    xi = x_index()
    outs = (g0, g1, g2, g3)
    grad = dot(act_ref[...], dy_ref[...].reshape(POS, CH), 1, 0)
    split_blocks(xi, grad, whole_ref, outs, 9 * OWN + 16)
    for g in range(8):
        lanes = slice(128 * g, 128 * (g + 1))
        came = [w2_ref[4 * g + j].astype(F32) for j in range(4)]
        for t in range(8):
            rows, at = slice(OWN * (t // 4), OWN * (t // 4 + 1)), OWN * (t % 4)
            parts = [v[rows, at : at + OWN] for v in came]
            w2t_ref[OWN * t : OWN * (t + 1), lanes] = jnp.concatenate(parts, axis=1).astype(BF)
        parts = [jnp.concatenate([v[2 * OWN :, OWN * a : OWN * (a + 1)] for v in came], axis=1) for a in range(4)]
        w2t_ref[8 * OWN :, lanes] = jnp.concatenate(parts, axis=0).astype(BF)
    products = dot(w2t_ref[...], dy_ref[...].reshape(POS, CH), 1, 1)
    act_grad = jnp.zeros((OWN, POS), F32)
    for t, (dr, dc) in enumerate(TAPS):
        act_grad = act_grad + shifted(products[OWN * t : OWN * (t + 1)], -dr, -dc)
    norm_grad = act_grad * slope
    gain_sum = jnp.sum(norm_grad * xhat, axis=1, keepdims=True)
    shift_sum = jnp.sum(norm_grad, axis=1, keepdims=True)
    scaled = norm_grad * gain
    count = 1.0 / (OWN * POS)
    first_mean = jnp.sum(scaled, keepdims=True) * count
    second_mean = jnp.sum(scaled * xhat, keepdims=True) * count
    pre_grad = rstd * (scaled - first_mean - xhat * second_mean)
    pre_grad = pre_grad.astype(BF).astype(F32)
    for t, (dr, dc) in enumerate(TAPS):
        taps_ref[OWN * t : OWN * (t + 1), :] = shifted(pre_grad, -dr, -dc)
    taps = taps_ref[...]
    grad = dot(taps.astype(BF), x_ref[...].reshape(POS, CH), 1, 0)
    split_blocks(xi, grad, whole_ref, outs, 0)
    high_g = gain_sum.astype(BF).astype(F32)
    high_s = shift_sum.astype(BF).astype(F32)
    lane = lax.broadcasted_iota(jnp.int32, (OWN, 128), 1)
    sums = jnp.where(lane == 0, high_g, 0.0) + jnp.where(lane == 1, gain_sum - high_g, 0.0)
    sums = sums + jnp.where(lane == 2, high_s, 0.0) + jnp.where(lane == 3, shift_sum - high_s, 0.0)
    extra = sums.T[:16, :]
    rows = slice(9 * OWN, 9 * OWN + 16)
    for out in outs:
        out[rows, :] = jnp.zeros((16, 256), out.dtype)
        out[rows, :OWN] = extra.astype(out.dtype)
    rows_ref[...] = taps.T
    half = len(SUM_ORDER) // 2
    for part, out in enumerate((p_near, p_far)):
        blocks = []
        for mask in SUM_ORDER[part * half : (part + 1) * half]:
            start = pl.multiple_of((me ^ mask) * ROWS, ROWS)
            blocks.append(rows_ref[pl.ds(start, ROWS), :])
        out[...] = dot(jnp.concatenate(blocks, axis=0).astype(BF), w1_ref[...], 1, 0)


def split_blocks(xi, grad, whole_ref, outs, at):
    whole_ref[...] = grad
    rows = slice(at, at + grad.shape[0])
    for m, out in enumerate(outs):
        lane = pl.multiple_of((xi ^ m) * 256, 256)
        out[rows, :] = whole_ref[:, pl.ds(lane, 256)].astype(out.dtype)


def turn_kernel(w_ref, out_ref):
    turned = w_ref[...].astype(F32).T
    last = turned[:, 256:].reshape(32, 4, 8, OWN)
    last = jnp.concatenate([last[:, a] for a in range(4)], axis=2)
    low, high = turned[:, :128].reshape(32, OWN, 128), turned[:, 128:256].reshape(32, OWN, 128)
    out_ref[...] = jnp.concatenate([low, high, last], axis=1).astype(BF)


def finish_kernel(a0, a1, a2, a3, first_ref, second_ref, gain_ref, shift_ref):
    xi = x_index()
    sums = jnp.zeros((16, 256), F32)
    for m, part in enumerate((a0, a1, a2, a3)):
        lanes = pl.ds(pl.multiple_of((xi ^ m) * 256, 256), 256)
        first_ref[:, lanes] = part[: 9 * OWN, :].astype(F32)
        second_ref[:, lanes] = part[9 * OWN + 16 :, :].astype(F32)
        sums = jnp.where(xi == m, part[9 * OWN : 9 * OWN + 16, :].astype(F32), sums)
    gain_ref[...] = sums[0:1, :OWN] + sums[1:2, :OWN]
    shift_ref[...] = sums[2:3, :OWN] + sums[3:4, :OWN]


LIMIT = 14 * MB


def call(kernel, operands, outs, scratch=(), flops=0):
    vmem = pl.BlockSpec(memory_space=pltpu.VMEM)
    return pl.pallas_call(
        kernel,
        out_shape=[jax.ShapeDtypeStruct(s, d) for s, d in outs],
        in_specs=[vmem] * len(operands),
        out_specs=[vmem] * len(outs),
        scratch_shapes=[pltpu.VMEM(s, d) for s, d in scratch],
        compiler_params=pltpu.CompilerParams(vmem_limit_bytes=LIMIT),
        cost_estimate=pl.CostEstimate(flops=flops, bytes_accessed=4 * MB, transcendentals=0),
    )(*operands)


def resplit(total):
    gain = total[9 * OWN : 9 * OWN + 1] + total[9 * OWN + 1 : 9 * OWN + 2]
    shift = total[9 * OWN + 2 : 9 * OWN + 3] + total[9 * OWN + 3 : 9 * OWN + 4]
    high_g, high_s = gain.astype(BF).astype(F32), shift.astype(BF).astype(F32)
    row = lax.broadcasted_iota(jnp.int32, (16, 256), 0)
    extra = jnp.where(row == 0, high_g, 0.0) + jnp.where(row == 1, gain - high_g, 0.0)
    extra = extra + jnp.where(row == 2, high_s, 0.0) + jnp.where(row == 3, shift - high_s, 0.0)
    return extra.astype(BF)


def x_sum_kernel(own_ref, r1, r2, r3, out_ref):
    total = own_ref[...] + r1[...].astype(F32) + r2[...].astype(F32) + r3[...].astype(F32)
    out_ref[...] = total.astype(BF)
    out_ref[9 * OWN : 9 * OWN + 16, :] = resplit(total)


def z_sum_kernel(mine_ref, other_ref, out_ref):
    total = mine_ref[...].astype(F32) + other_ref[...].astype(F32)
    out_ref[...] = total.astype(BF)
    out_ref[9 * OWN : 9 * OWN + 16, :] = resplit(total)


def x_hops(parts):
    return [parts[0]] + [hop(parts[m], 2 * m, "sample", 8) for m in (1, 2, 3)]


def z_hop(mine):
    return hop(mine, 1, "sample", 8)


def spread(mine):
    return [mine] + [hop(mine, 2 * m, "sample", 8) for m in (1, 2, 3)]


def after(value, *others):
    return lax.optimization_barrier((value, *others))[0]


def per_device(inputs, first_weight, second_weight, norm_gain_vector, norm_bias, cotangent):
    w2 = second_weight.reshape(9 * OWN, CH)
    (turned,) = call(turn_kernel, [w2], [((32, 72, 128), BF)])
    block = jnp.concatenate([inputs.reshape(1, ROWS, CH), cotangent.reshape(1, ROWS, CH)], axis=1)
    held = jnp.concatenate([block] + [hop(block, m) for m in Z_MASKS])
    got = [hop(held, m) for m in Y_MASKS]
    w2_own = lax.all_to_all(after(turned, held), "tile", split_axis=0, concat_axis=0, tiled=True)
    near = jnp.concatenate([held] + got)
    far = hop(near, CORE)
    w1 = first_weight.reshape(9 * OWN, CH)
    gain, bias = norm_gain_vector.reshape(1, OWN), norm_bias.reshape(1, OWN)
    flops = 2 * 288 * POS * CH
    columns, taps, whole = (COLS, ROWS, CH), (9 * OWN, POS), (9 * OWN, CH)
    joint = (18 * OWN + 16, 256)
    (state,) = call(forward_kernel, [near, far, w1], [((OWN + 8, POS), F32)], [(columns, BF)], flops)
    conv_near, conv_far, *parts = call(
        main_kernel,
        [near, far, w2_own, w1, gain, bias, state],
        [((POS // 2, CH), F32)] * 2 + [(joint, F32)] + [(joint, BF)] * 3,
        [(columns, BF), (columns, BF), (taps, BF), (whole, BF), (taps, F32), ((POS, 9 * OWN), F32), (whole, F32)],
        4 * flops,
    )
    parts = x_hops(parts)
    conv_far = hop(conv_far, CORE)
    total = (conv_near + conv_far).reshape(4, POS // 8, CH)
    y_got = [hop(total[k].astype(BF), m) for k, m in zip((1, 2, 3), Y_MASKS)]
    (mine,) = call(x_sum_kernel, [after(parts[0], *y_got), *parts[1:]], [(joint, BF)])
    other = z_hop(mine)
    total = total[0] + y_got[0].astype(F32) + y_got[1].astype(F32) + y_got[2].astype(F32)
    total = after(total.reshape(4, ROWS, CH), other)
    z_got = [hop(total[k].astype(BF), m) for k, m in zip((1, 2, 3), Z_MASKS)]
    (summed,) = call(z_sum_kernel, [mine, other], [(joint, BF)])
    blocks = spread(summed)
    total = total[0] + z_got[0].astype(F32) + z_got[1].astype(F32) + z_got[2].astype(F32)
    conv_back = total.astype(BF).astype(F32)
    input_grad = (cotangent.reshape(ROWS, CH).astype(F32) + conv_back).astype(BF)
    grad, row = ((9 * OWN, CH), F32), ((1, OWN), F32)
    first_grad, second_grad, gain_grad, shift_grad = call(finish_kernel, blocks, [grad, grad, row, row])
    return (
        input_grad.reshape(1, ROWS, 1, CH),
        first_grad.reshape(9, OWN, CH),
        jnp.transpose(second_grad.reshape(9, OWN, CH), (0, 2, 1)),
        gain_grad.reshape(OWN),
        shift_grad.reshape(OWN),
    )


def solution(mesh):
    return jax.shard_map(
        per_device,
        mesh=mesh,
        in_specs=(
            P("sample", None, "tile", None),
            P(None, "tile", None),
            P(None, "tile", None),
            P("tile"),
            P("tile"),
            P("sample", None, "tile", None),
        ),
        out_specs=(
            P("sample", None, "tile", None),
            P(None, "tile", None),
            P(None, None, "tile"),
            P("tile"),
            P("tile"),
        ),
        check_vma=False,
    )
```

profile of v0, /device:TPU:32, one launch (start us, length us, event | category | flops | bytes accessed | tf_op | source)
XLA Modules:
  0.0 99.7 jit_solution(18028982534716995799)
XLA Ops:
  0.6 0.0 copy-start.4
  0.6 0.0 copy-start.5
  0.7 0.8 pad_maximum_fusion.1
  1.5 3.4 %collective-permute-start.1 = (bf16[1,32,1024]{2,1,0:T(8,128)(2,1)S(1)}, bf16[1,32,1024]{2,1,0:T(8,128)(2,1)S(1)}, u32[]{:S(2)}, u32[]{:S(2)}) collective-permute-start(bf16[1,32,1024]{2,1,0:T(8,128)(2,1)S(1)} %get-tuple-element.39), channel_id=1, source_target_pairs={{0,128},{8,136},{16,144},{24,152},{32,160},{40,168},{48,176},{56,1... | collective-permute-start | bytes 196616 | tf_op jit(solution)/shard_map/ppermute | solution.py:24
  4.8 0.1 collective-permute-start
  5.0 0.6 collective-permute-start.2
  5.5 0.0 copy-start
  5.5 1.1 %copy-done = bf16[9,32,1024]{2,1,0:T(8,128)(2,1)S(1)} copy-done((bf16[9,32,1024]{2,1,0:T(8,128)(2,1)S(1)}, bf16[9,32,1024]{2,1,0:T(8,128)(2,1)}, u32[]{:S(2)}) %copy-start) | copy-done | bytes 589848
  6.6 1.2 %shard_map.101 = bf16[32,72,128]{2,1,0:T(8,128)(2,1)} custom-call(bf16[288,1024]{1,0:T(8,128)(2,1)S(1)} %bitcast.36), custom_call_target="tpu_custom_call" | custom-call | bytes 4194304 | tf_op jit(solution)/shard_map/pallas_call | solution.py:174
  7.8 0.4 collective-permute-done.1
  8.1 1.1 %collective-permute-done = bf16[1,32,1024]{2,1,0:T(8,128)(2,1)S(1)} collective-permute-done((bf16[1,32,1024]{2,1,0:T(8,128)(2,1)S(1)}, bf16[1,32,1024]{2,1,0:T(8,128)(2,1)S(1)}, u32[]{:S(2)}, u32[]{:S(2)}) %collective-permute-start) | collective-permute-done | bytes 65568 | tf_op jit(solution)/shard_map/ppermute | solution.py:24
  9.3 0.7 collective-permute-done.2
  10.0 0.0 copy-done.4
  10.0 0.0 copy-done.5
  10.0 3.1 %collective-permute-start.5 = (bf16[4,32,1024]{2,1,0:T(8,128)(2,1)S(1)}, bf16[4,32,1024]{2,1,0:T(8,128)(2,1)S(1)}, u32[]{:S(2)}, u32[]{:S(2)}) collective-permute-start(bf16[4,32,1024]{2,1,0:T(8,128)(2,1)S(1)} %pad_maximum_fusion), channel_id=1, source_target_pairs={{0,48},{8,56},{16,32},{24,40},{32,16},{40,24},{48,0},{56,8},{64,11... | collective-permute-start | bytes 786440 | tf_op jit(solution)/shard_map/ppermute | solution.py:24
  13.1 0.6 collective-permute-start.4
  13.7 0.5 collective-permute-start.3
  14.2 8.0 %all-to-all-start = ((bf16[32,72,128]{2,1,0:T(8,128)(2,1)}), bf16[32,72,128]{2,1,0:T(8,128)(2,1)S(1)}, u32[]{:S(2)}, u32[]{:S(2)}) async-start(bf16[32,72,128]{2,1,0:T(8,128)(2,1)} %shard_map.101), calls=%async_computation | async-start | bytes 1179648 | tf_op jit(solution)/shard_map/all_to_all | solution.py:229
  22.2 0.0 copy-start.1
  22.3 4.7 %collective-permute-done.3 = bf16[4,32,1024]{2,1,0:T(8,128)(2,1)S(1)} collective-permute-done((bf16[4,32,1024]{2,1,0:T(8,128)(2,1)S(1)}, bf16[4,32,1024]{2,1,0:T(8,128)(2,1)S(1)}, u32[]{:S(2)}, u32[]{:S(2)}) %collective-permute-start.3) | collective-permute-done | bytes 262176 | tf_op jit(solution)/shard_map/ppermute | solution.py:24
  27.0 0.0 collective-permute-done.4
  27.0 0.0 collective-permute-done.5
  27.1 0.1 collective-permute-start.6
  27.2 2.6 %collective-permute-done.6.far_ref = bf16[16,32,1024]{2,1,0:T(8,128)(2,1)S(1)} collective-permute-done((bf16[16,32,1024]{2,1,0:T(8,128)(2,1)S(1)}, bf16[16,32,1024]{2,1,0:T(8,128)(2,1)S(1)}, u32[]{:S(2)}, u32[]{:S(2)}) %collective-permute-start.6) | collective-permute-done | bytes 1048608 | tf_op jit(solution)/shard_map/ppermute | solution.py:24
  29.8 0.0 copy-done.1
  29.8 1.0 shard_map.102.state_ref
  30.8 8.0 %all-to-all-done.w2_ref = bf16[32,72,128]{2,1,0:T(8,128)(2,1)S(1)} async-done(((bf16[32,72,128]{2,1,0:T(8,128)(2,1)}), bf16[32,72,128]{2,1,0:T(8,128)(2,1)S(1)}, u32[]{:S(2)}, u32[]{:S(2)}) %all-to-all-start) | async-done | bytes 589856 | tf_op jit(solution)/shard_map/all_to_all | solution.py:229
  38.8 0.0 copy-done.2
  38.8 0.0 copy-done.3
  38.8 2.5 %shard_map.103 = (f32[256,1024]{1,0:T(8,128)S(1)}, f32[256,1024]{1,0:T(8,128)S(1)}, f32[592,256]{1,0:T(8,128)S(1)}, bf16[592,256]{1,0:T(8,128)(2,1)S(1)}, bf16[5...) custom-call(bf16[16,32,1024]{2,1,0:T(8,128)(2,1)S(1)} %constant_dynamic-update-slice_fusion.near_ref, ...), custom_call_target="tpu_custom_call" | custom-call | flops 1207959552 | bytes 4194304 | tf_op jit(solution)/shard_map/pallas_call | solution.py:174
  41.3 0.7 collective-permute-start.7
  42.0 1.5 %collective-permute-start.11 = (bf16[592,256]{1,0:T(8,128)(2,1)S(1)}, bf16[592,256]{1,0:T(8,128)(2,1)S(1)}, u32[]{:S(2)}, u32[]{:S(2)}) collective-permute-start(bf16[592,256]{1,0:T(8,128)(2,1)S(1)} %get-tuple-element.23), channel_id=1, source_target_pairs={{0,2},{1,3},{2,0},{3,1},{4,6},{5,7},{6,4},{7,5},{8,10},{9,11},{10,... | collective-permute-start | bytes 909320 | tf_op jit(solution)/shard_map/ppermute | solution.py:24
  43.5 2.7 %collective-permute-start.12 = (bf16[592,256]{1,0:T(8,128)(2,1)S(1)}, bf16[592,256]{1,0:T(8,128)(2,1)S(1)}, u32[]{:S(2)}, u32[]{:S(2)}) collective-permute-start(bf16[592,256]{1,0:T(8,128)(2,1)S(1)} %get-tuple-element.24), channel_id=1, source_target_pairs={{0,4},{1,5},{2,6},{3,7},{4,0},{5,1},{6,2},{7,3},{8,12},{9,13},{10,... | collective-permute-start | bytes 909320 | tf_op jit(solution)/shard_map/ppermute | solution.py:24
  46.2 0.5 collective-permute-start.13
  46.7 0.0 collective-permute-done.7
  46.7 0.2 fusion.7
  47.0 0.7 collective-permute-start.8
  47.6 0.8 collective-permute-start.10
  48.4 3.6 %collective-permute-done.8 = bf16[64,1024]{1,0:T(8,128)(2,1)S(1)} collective-permute-done((bf16[64,1024]{1,0:T(8,128)(2,1)S(1)}, bf16[64,1024]{1,0:T(8,128)(2,1)S(1)}, u32[]{:S(2)}, u32[]{:S(2)}) %collective-permute-start.8) | collective-permute-done | bytes 131104 | tf_op jit(solution)/shard_map/ppermute | solution.py:24
  52.0 0.8 collective-permute-start.9
  52.8 1.0 collective-permute-done.10
  53.8 4.7 %collective-permute-done.9 = bf16[64,1024]{1,0:T(8,128)(2,1)S(1)} collective-permute-done((bf16[64,1024]{1,0:T(8,128)(2,1)S(1)}, bf16[64,1024]{1,0:T(8,128)(2,1)S(1)}, u32[]{:S(2)}, u32[]{:S(2)}) %collective-permute-start.9) | collective-permute-done | bytes 131104 | tf_op jit(solution)/shard_map/ppermute | solution.py:24
  58.5 0.0 collective-permute-done.11.r1
  58.5 1.5 %collective-permute-done.12.r2 = bf16[592,256]{1,0:T(8,128)(2,1)S(1)} collective-permute-done((bf16[592,256]{1,0:T(8,128)(2,1)S(1)}, bf16[592,256]{1,0:T(8,128)(2,1)S(1)}, u32[]{:S(2)}, u32[]{:S(2)}) %collective-permute-start.12) | collective-permute-done | bytes 303136 | tf_op jit(solution)/shard_map/ppermute | solution.py:24
  60.0 2.6 %collective-permute-done.13.r3 = bf16[592,256]{1,0:T(8,128)(2,1)S(1)} collective-permute-done((bf16[592,256]{1,0:T(8,128)(2,1)S(1)}, bf16[592,256]{1,0:T(8,128)(2,1)S(1)}, u32[]{:S(2)}, u32[]{:S(2)}) %collective-permute-start.13) | collective-permute-done | bytes 303136 | tf_op jit(solution)/shard_map/ppermute | solution.py:24
  62.6 0.2 shard_map.104.mine_ref
  62.7 5.8 %collective-permute-start.14 = (bf16[592,256]{1,0:T(8,128)(2,1)S(1)}, bf16[592,256]{1,0:T(8,128)(2,1)S(1)}, u32[]{:S(2)}, u32[]{:S(2)}) collective-permute-start(bf16[592,256]{1,0:T(8,128)(2,1)S(1)} %shard_map.104.mine_ref), channel_id=1, source_target_pairs={{0,1},{1,0},{2,3},{3,2},{4,5},{5,4},{6,7},{7,6},{8,9},{9,8},{10,11... | collective-permute-start | bytes 909320 | tf_op jit(solution)/shard_map/ppermute | solution.py:24
  68.5 0.1 fusion.1
  68.5 12.7 %collective-permute-done.14.other_ref = bf16[592,256]{1,0:T(8,128)(2,1)S(1)} collective-permute-done((bf16[592,256]{1,0:T(8,128)(2,1)S(1)}, bf16[592,256]{1,0:T(8,128)(2,1)S(1)}, u32[]{:S(2)}, u32[]{:S(2)}) %collective-permute-start.14) | collective-permute-done | bytes 303136 | tf_op jit(solution)/shard_map/ppermute | solution.py:24
  81.2 0.1 shard_map.105.a0
  81.3 0.6 collective-permute-start.20
  81.9 0.0 collective-permute-start.19
  81.9 3.6 %collective-permute-start.18 = (bf16[592,256]{1,0:T(8,128)(2,1)S(1)}, bf16[592,256]{1,0:T(8,128)(2,1)S(1)}, u32[]{:S(2)}, u32[]{:S(2)}) collective-permute-start(bf16[592,256]{1,0:T(8,128)(2,1)S(1)} %shard_map.105.a0), channel_id=1, source_target_pairs={{0,2},{1,3},{2,0},{3,1},{4,6},{5,7},{6,4},{7,5},{8,10},{9,11},{10,... | collective-permute-start | bytes 909320 | tf_op jit(solution)/shard_map/ppermute | solution.py:24
  85.5 0.1 collective-permute-start.15
  85.6 1.3 %collective-permute-start.17 = (bf16[16,1024]{1,0:T(8,128)(2,1)S(1)}, bf16[16,1024]{1,0:T(8,128)(2,1)S(1)}, u32[]{:S(2)}, u32[]{:S(2)}) collective-permute-start(bf16[16,1024]{1,0:T(8,128)(2,1)S(1)} %get-tuple-element.37), channel_id=1, source_target_pairs={{0,192},{8,200},{16,208},{24,216},{32,224},{40,232},{48,240},{56,2... | collective-permute-start | bytes 98312 | tf_op jit(solution)/shard_map/ppermute | solution.py:24
  86.9 2.6 %collective-permute-done.15 = bf16[16,1024]{1,0:T(8,128)(2,1)S(1)} collective-permute-done((bf16[16,1024]{1,0:T(8,128)(2,1)S(1)}, bf16[16,1024]{1,0:T(8,128)(2,1)S(1)}, u32[]{:S(2)}, u32[]{:S(2)}) %collective-permute-start.15) | collective-permute-done | bytes 32800 | tf_op jit(solution)/shard_map/ppermute | solution.py:24
  89.5 0.6 collective-permute-start.16
  90.2 0.0 collective-permute-done.17
  90.2 4.2 %collective-permute-done.16 = bf16[16,1024]{1,0:T(8,128)(2,1)S(1)} collective-permute-done((bf16[16,1024]{1,0:T(8,128)(2,1)S(1)}, bf16[16,1024]{1,0:T(8,128)(2,1)S(1)}, u32[]{:S(2)}, u32[]{:S(2)}) %collective-permute-start.16) | collective-permute-done | bytes 32800 | tf_op jit(solution)/shard_map/ppermute | solution.py:24
  94.3 0.6 fusion.6
  95.0 2.6 %collective-permute-done.20.a3 = bf16[592,256]{1,0:T(8,128)(2,1)S(1)} collective-permute-done((bf16[592,256]{1,0:T(8,128)(2,1)S(1)}, bf16[592,256]{1,0:T(8,128)(2,1)S(1)}, u32[]{:S(2)}, u32[]{:S(2)}) %collective-permute-start.20) | collective-permute-done | bytes 303136 | tf_op jit(solution)/shard_map/ppermute | solution.py:24
  97.6 0.0 collective-permute-done.19.a2
  97.6 0.6 collective-permute-done.18.a1
  98.2 1.6 %shard_map.106 = (f32[288,1024]{1,0:T(8,128)}, f32[288,1024]{1,0:T(8,128)}, f32[1,32]{1,0:T(1,128)}, f32[1,32]{1,0:T(1,128)}) custom-call(bf16[592,256]{1,0:T(8,128)(2,1)S(1)} %shard_map.105.a0, bf16[592,256]{1,0:T(8,128)(2,1)S(1)} %collective-permute-done.18.a1, bf16[592,256]{1,0:T(8,128)(2,1)S(1)} %collective-permute-done.19.a2, ...), custom_call_target="tpu_custom_call" | custom-call | bytes 4194304 | tf_op jit(solution)/shard_map/pallas_call | solution.py:174
  (12 shorter events, 0.1 us)
Async XLA Ops:
  0.6 9.3 %copy-start.4 = (bf16[1,16,1,1024]{3,1,2,0:T(8,128)(2,1)S(1)}, bf16[1,16,1,1024]{3,1,2,0:T(8,128)(2,1)}, u32[]{:S(2)}) copy-start(bf16[1,16,1,1024]{3,1,2,0:T(8,128)(2,1)} %param.11) | copy-start | bytes 98308
  0.6 9.3 %copy-start.5 = (bf16[1,16,1,1024]{3,1,2,0:T(8,128)(2,1)S(1)}, bf16[1,16,1,1024]{3,1,2,0:T(8,128)(2,1)}, u32[]{:S(2)}) copy-start(bf16[1,16,1,1024]{3,1,2,0:T(8,128)(2,1)} %param.6) | copy-start | bytes 98308
  1.5 6.7 %collective-permute-start.1 = (bf16[1,32,1024]{2,1,0:T(8,128)(2,1)S(1)}, bf16[1,32,1024]{2,1,0:T(8,128)(2,1)S(1)}, u32[]{:S(2)}, u32[]{:S(2)}) collective-permute-start(bf16[1,32,1024]{2,1,0:T(8,128)(2,1)S(1)} %get-tuple-element.39), channel_id=1, source_target_pairs={{0,128},{8,136},{16,144},{24,152},{32,160},{40,168},{48,176},{56,1... | collective-permute-start | bytes 196616 | tf_op jit(solution)/shard_map/ppermute | solution.py:24
  4.8 4.5 %collective-permute-start = (bf16[1,32,1024]{2,1,0:T(8,128)(2,1)S(1)}, bf16[1,32,1024]{2,1,0:T(8,128)(2,1)S(1)}, u32[]{:S(2)}, u32[]{:S(2)}) collective-permute-start(bf16[1,32,1024]{2,1,0:T(8,128)(2,1)S(1)} %get-tuple-element.39), channel_id=1, source_target_pairs={{0,64},{8,72},{16,80},{24,88},{32,96},{40,104},{48,112},{56,120},{... | collective-permute-start | bytes 196616 | tf_op jit(solution)/shard_map/ppermute | solution.py:24
  5.0 5.0 %collective-permute-start.2 = (bf16[1,32,1024]{2,1,0:T(8,128)(2,1)S(1)}, bf16[1,32,1024]{2,1,0:T(8,128)(2,1)S(1)}, u32[]{:S(2)}, u32[]{:S(2)}) collective-permute-start(bf16[1,32,1024]{2,1,0:T(8,128)(2,1)S(1)} %get-tuple-element.39), channel_id=1, source_target_pairs={{0,192},{8,200},{16,208},{24,216},{32,224},{40,232},{48,240},{56,2... | collective-permute-start | bytes 196616 | tf_op jit(solution)/shard_map/ppermute | solution.py:24
  5.5 1.1 %copy-start = (bf16[9,32,1024]{2,1,0:T(8,128)(2,1)S(1)}, bf16[9,32,1024]{2,1,0:T(8,128)(2,1)}, u32[]{:S(2)}) copy-start(bf16[9,32,1024]{2,1,0:T(8,128)(2,1)} %param.8) | copy-start | bytes 1769476
  10.0 17.1 %collective-permute-start.5 = (bf16[4,32,1024]{2,1,0:T(8,128)(2,1)S(1)}, bf16[4,32,1024]{2,1,0:T(8,128)(2,1)S(1)}, u32[]{:S(2)}, u32[]{:S(2)}) collective-permute-start(bf16[4,32,1024]{2,1,0:T(8,128)(2,1)S(1)} %pad_maximum_fusion), channel_id=1, source_target_pairs={{0,48},{8,56},{16,32},{24,40},{32,16},{40,24},{48,0},{56,8},{64,11... | collective-permute-start | bytes 786440 | tf_op jit(solution)/shard_map/ppermute | solution.py:24
  13.1 13.9 %collective-permute-start.4 = (bf16[4,32,1024]{2,1,0:T(8,128)(2,1)S(1)}, bf16[4,32,1024]{2,1,0:T(8,128)(2,1)S(1)}, u32[]{:S(2)}, u32[]{:S(2)}) collective-permute-start(bf16[4,32,1024]{2,1,0:T(8,128)(2,1)S(1)} %pad_maximum_fusion), channel_id=1, source_target_pairs={{0,32},{8,40},{16,48},{24,56},{32,0},{40,8},{48,16},{56,24},{64,96... | collective-permute-start | bytes 786440 | tf_op jit(solution)/shard_map/ppermute | solution.py:24
  13.7 13.3 %collective-permute-start.3 = (bf16[4,32,1024]{2,1,0:T(8,128)(2,1)S(1)}, bf16[4,32,1024]{2,1,0:T(8,128)(2,1)S(1)}, u32[]{:S(2)}, u32[]{:S(2)}) collective-permute-start(bf16[4,32,1024]{2,1,0:T(8,128)(2,1)S(1)} %pad_maximum_fusion), channel_id=1, source_target_pairs={{0,16},{8,24},{16,0},{24,8},{32,48},{40,56},{48,32},{56,40},{64,80... | collective-permute-start | bytes 786440 | tf_op jit(solution)/shard_map/ppermute | solution.py:24
  14.2 24.7 %all-to-all-start = ((bf16[32,72,128]{2,1,0:T(8,128)(2,1)}), bf16[32,72,128]{2,1,0:T(8,128)(2,1)S(1)}, u32[]{:S(2)}, u32[]{:S(2)}) async-start(bf16[32,72,128]{2,1,0:T(8,128)(2,1)} %shard_map.101), calls=%async_computation | async-start | bytes 1179648 | tf_op jit(solution)/shard_map/all_to_all | solution.py:229
  22.2 7.6 %copy-start.1 = (bf16[9,32,1024]{2,1,0:T(8,128)(2,1)S(1)}, bf16[9,32,1024]{2,1,0:T(8,128)(2,1)}, u32[]{:S(2)}) copy-start(bf16[9,32,1024]{2,1,0:T(8,128)(2,1)} %param.7) | copy-start | bytes 1769476
  27.1 2.7 %collective-permute-start.6 = (bf16[16,32,1024]{2,1,0:T(8,128)(2,1)S(1)}, bf16[16,32,1024]{2,1,0:T(8,128)(2,1)S(1)}, u32[]{:S(2)}, u32[]{:S(2)}) collective-permute-start(bf16[16,32,1024]{2,1,0:T(8,128)(2,1)S(1)} %constant_dynamic-update-slice_fusion.near_ref), channel_id=1, source_target_pairs={{0,8},{8,0},{16,24},{24,16},{32,40},{40,32},{48,56},{56,48},{64,72... | collective-permute-start | bytes 3145736 | tf_op jit(solution)/shard_map/ppermute | solution.py:24
  29.8 9.0 %copy-start.2 = (f32[32]{0:T(128)S(1)}, f32[32]{0:T(128)}, u32[]{:S(2)}) copy-start(f32[32]{0:T(128)} %param.9) | copy-start | bytes 388
  29.8 9.0 %copy-start.3 = (f32[32]{0:T(128)S(1)}, f32[32]{0:T(128)}, u32[]{:S(2)}) copy-start(f32[32]{0:T(128)} %param.10) | copy-start | bytes 388
  41.3 5.4 %collective-permute-start.7 = (f32[256,1024]{1,0:T(8,128)S(1)}, f32[256,1024]{1,0:T(8,128)S(1)}, u32[]{:S(2)}, u32[]{:S(2)}) collective-permute-start(f32[256,1024]{1,0:T(8,128)S(1)} %get-tuple-element.20), channel_id=1, source_target_pairs={{0,8},{8,0},{16,24},{24,16},{32,40},{40,32},{48,56},{56,48},{64,72... | collective-permute-start | bytes 3145736 | tf_op jit(solution)/shard_map/ppermute | solution.py:24
  42.0 16.5 %collective-permute-start.11 = (bf16[592,256]{1,0:T(8,128)(2,1)S(1)}, bf16[592,256]{1,0:T(8,128)(2,1)S(1)}, u32[]{:S(2)}, u32[]{:S(2)}) collective-permute-start(bf16[592,256]{1,0:T(8,128)(2,1)S(1)} %get-tuple-element.23), channel_id=1, source_target_pairs={{0,2},{1,3},{2,0},{3,1},{4,6},{5,7},{6,4},{7,5},{8,10},{9,11},{10,... | collective-permute-start | bytes 909320 | tf_op jit(solution)/shard_map/ppermute | solution.py:24
  43.5 16.5 %collective-permute-start.12 = (bf16[592,256]{1,0:T(8,128)(2,1)S(1)}, bf16[592,256]{1,0:T(8,128)(2,1)S(1)}, u32[]{:S(2)}, u32[]{:S(2)}) collective-permute-start(bf16[592,256]{1,0:T(8,128)(2,1)S(1)} %get-tuple-element.24), channel_id=1, source_target_pairs={{0,4},{1,5},{2,6},{3,7},{4,0},{5,1},{6,2},{7,3},{8,12},{9,13},{10,... | collective-permute-start | bytes 909320 | tf_op jit(solution)/shard_map/ppermute | solution.py:24
  46.2 16.3 %collective-permute-start.13 = (bf16[592,256]{1,0:T(8,128)(2,1)S(1)}, bf16[592,256]{1,0:T(8,128)(2,1)S(1)}, u32[]{:S(2)}, u32[]{:S(2)}) collective-permute-start(bf16[592,256]{1,0:T(8,128)(2,1)S(1)} %get-tuple-element.25), channel_id=1, source_target_pairs={{0,6},{1,7},{2,4},{3,5},{4,2},{5,3},{6,0},{7,1},{8,14},{9,15},{10,... | collective-permute-start | bytes 909320 | tf_op jit(solution)/shard_map/ppermute | solution.py:24
  47.0 5.1 %collective-permute-start.8 = (bf16[64,1024]{1,0:T(8,128)(2,1)S(1)}, bf16[64,1024]{1,0:T(8,128)(2,1)S(1)}, u32[]{:S(2)}, u32[]{:S(2)}) collective-permute-start(bf16[64,1024]{1,0:T(8,128)(2,1)S(1)} %get-tuple-element.33), channel_id=1, source_target_pairs={{0,16},{8,24},{16,0},{24,8},{32,48},{40,56},{48,32},{56,40},{64,80... | collective-permute-start | bytes 393224 | tf_op jit(solution)/shard_map/ppermute | solution.py:24
  47.6 6.2 %collective-permute-start.10 = (bf16[64,1024]{1,0:T(8,128)(2,1)S(1)}, bf16[64,1024]{1,0:T(8,128)(2,1)S(1)}, u32[]{:S(2)}, u32[]{:S(2)}) collective-permute-start(bf16[64,1024]{1,0:T(8,128)(2,1)S(1)} %get-tuple-element.34), channel_id=1, source_target_pairs={{0,48},{8,56},{16,32},{24,40},{32,16},{40,24},{48,0},{56,8},{64,11... | collective-permute-start | bytes 393224 | tf_op jit(solution)/shard_map/ppermute | solution.py:24
  52.0 6.5 %collective-permute-start.9 = (bf16[64,1024]{1,0:T(8,128)(2,1)S(1)}, bf16[64,1024]{1,0:T(8,128)(2,1)S(1)}, u32[]{:S(2)}, u32[]{:S(2)}) collective-permute-start(bf16[64,1024]{1,0:T(8,128)(2,1)S(1)} %get-tuple-element.35), channel_id=1, source_target_pairs={{0,32},{8,40},{16,48},{24,56},{32,0},{40,8},{48,16},{56,24},{64,96... | collective-permute-start | bytes 393224 | tf_op jit(solution)/shard_map/ppermute | solution.py:24
  62.7 18.5 %collective-permute-start.14 = (bf16[592,256]{1,0:T(8,128)(2,1)S(1)}, bf16[592,256]{1,0:T(8,128)(2,1)S(1)}, u32[]{:S(2)}, u32[]{:S(2)}) collective-permute-start(bf16[592,256]{1,0:T(8,128)(2,1)S(1)} %shard_map.104.mine_ref), channel_id=1, source_target_pairs={{0,1},{1,0},{2,3},{3,2},{4,5},{5,4},{6,7},{7,6},{8,9},{9,8},{10,11... | collective-permute-start | bytes 909320 | tf_op jit(solution)/shard_map/ppermute | solution.py:24
  81.3 16.3 %collective-permute-start.20 = (bf16[592,256]{1,0:T(8,128)(2,1)S(1)}, bf16[592,256]{1,0:T(8,128)(2,1)S(1)}, u32[]{:S(2)}, u32[]{:S(2)}) collective-permute-start(bf16[592,256]{1,0:T(8,128)(2,1)S(1)} %shard_map.105.a0), channel_id=1, source_target_pairs={{0,6},{1,7},{2,4},{3,5},{4,2},{5,3},{6,0},{7,1},{8,14},{9,15},{10,... | collective-permute-start | bytes 909320 | tf_op jit(solution)/shard_map/ppermute | solution.py:24
  81.9 15.7 %collective-permute-start.19 = (bf16[592,256]{1,0:T(8,128)(2,1)S(1)}, bf16[592,256]{1,0:T(8,128)(2,1)S(1)}, u32[]{:S(2)}, u32[]{:S(2)}) collective-permute-start(bf16[592,256]{1,0:T(8,128)(2,1)S(1)} %shard_map.105.a0), channel_id=1, source_target_pairs={{0,4},{1,5},{2,6},{3,7},{4,0},{5,1},{6,2},{7,3},{8,12},{9,13},{10,... | collective-permute-start | bytes 909320 | tf_op jit(solution)/shard_map/ppermute | solution.py:24
  81.9 16.3 %collective-permute-start.18 = (bf16[592,256]{1,0:T(8,128)(2,1)S(1)}, bf16[592,256]{1,0:T(8,128)(2,1)S(1)}, u32[]{:S(2)}, u32[]{:S(2)}) collective-permute-start(bf16[592,256]{1,0:T(8,128)(2,1)S(1)} %shard_map.105.a0), channel_id=1, source_target_pairs={{0,2},{1,3},{2,0},{3,1},{4,6},{5,7},{6,4},{7,5},{8,10},{9,11},{10,... | collective-permute-start | bytes 909320 | tf_op jit(solution)/shard_map/ppermute | solution.py:24
  85.5 4.0 %collective-permute-start.15 = (bf16[16,1024]{1,0:T(8,128)(2,1)S(1)}, bf16[16,1024]{1,0:T(8,128)(2,1)S(1)}, u32[]{:S(2)}, u32[]{:S(2)}) collective-permute-start(bf16[16,1024]{1,0:T(8,128)(2,1)S(1)} %get-tuple-element.36), channel_id=1, source_target_pairs={{0,64},{8,72},{16,80},{24,88},{32,96},{40,104},{48,112},{56,120},{... | collective-permute-start | bytes 98312 | tf_op jit(solution)/shard_map/ppermute | solution.py:24
  85.6 4.5 %collective-permute-start.17 = (bf16[16,1024]{1,0:T(8,128)(2,1)S(1)}, bf16[16,1024]{1,0:T(8,128)(2,1)S(1)}, u32[]{:S(2)}, u32[]{:S(2)}) collective-permute-start(bf16[16,1024]{1,0:T(8,128)(2,1)S(1)} %get-tuple-element.37), channel_id=1, source_target_pairs={{0,192},{8,200},{16,208},{24,216},{32,224},{40,232},{48,240},{56,2... | collective-permute-start | bytes 98312 | tf_op jit(solution)/shard_map/ppermute | solution.py:24
  89.5 4.8 %collective-permute-start.16 = (bf16[16,1024]{1,0:T(8,128)(2,1)S(1)}, bf16[16,1024]{1,0:T(8,128)(2,1)S(1)}, u32[]{:S(2)}, u32[]{:S(2)}) collective-permute-start(bf16[16,1024]{1,0:T(8,128)(2,1)S(1)} %get-tuple-element.38), channel_id=1, source_target_pairs={{0,128},{8,136},{16,144},{24,152},{32,160},{40,168},{48,176},{56,1... | collective-permute-start | bytes 98312 | tf_op jit(solution)/shard_map/ppermute | solution.py:24
where the time goes:
time: 100 us; the launch traced here: 99.7 us
  waiting for transfers between devices  53.6 us (54%)
  starting transfers between devices  35.9 us (36%)
  Pallas kernels  6.4 us (6%)
  other arithmetic  1.79 us (2%)
  local copies, waits for them, and re-layouts  1.2 us (1%)
    ppermute x21, waiting for transfers between devices, hop(): return lax.ppermute(value, axis, [(i, i ^ mask) for i in range(size)])  45.6 us
    ppermute x21, starting transfers between devices, hop(): return lax.ppermute(value, axis, [(i, i ^ mask) for i in range(size)])  27.9 us
    all_to_all x1, starting transfers between devices, per_device(): lax.all_to_all(after(turned, held), 'tile', split_axis=0, concat_axis=0,...  8.04 us
    all_to_all x1, waiting for transfers between devices, per_device(): lax.all_to_all(after(turned, held), 'tile', split_axis=0, concat_axis=0,...  8.02 us
    pallas_call x6, Pallas kernels, call(): pl.pallas_call(kernel, out_shape=[jax.ShapeDtypeStruct(s, d) for s, d in...  6.4 us
  transfers between devices with their start and end apart: 22, of which 16 were waited for; matrix products, arithmetic and copies ran while one was open for 1% of the time, Pallas kernels for 2%

commit v1 on v0

--- a/solution.py
+++ b/solution.py
@@ -246,12 +246,12 @@
     conv_far = hop(conv_far, CORE)
     total = (conv_near + conv_far).reshape(4, POS // 8, CH)
     y_got = [hop(total[k].astype(BF), m) for k, m in zip((1, 2, 3), Y_MASKS)]
-    (mine,) = call(x_sum_kernel, [after(parts[0], *y_got), *parts[1:]], [(joint, BF)])
+    (mine,) = call(x_sum_kernel, parts, [(joint, BF)])
     other = z_hop(mine)
     total = total[0] + y_got[0].astype(F32) + y_got[1].astype(F32) + y_got[2].astype(F32)
     total = after(total.reshape(4, ROWS, CH), other)
     z_got = [hop(total[k].astype(BF), m) for k, m in zip((1, 2, 3), Z_MASKS)]
-    (summed,) = call(z_sum_kernel, [mine, other], [(joint, BF)])
+    (summed,) = call(z_sum_kernel, [after(mine, *y_got), other], [(joint, BF)])
     blocks = spread(summed)
     total = total[0] + z_got[0].astype(F32) + z_got[1].astype(F32) + z_got[2].astype(F32)
     conv_back = total.astype(BF).astype(F32)

time: 100 us -> 99.9 us (level)
  waiting for transfers between devices: 53.6 us -> 51.7 us
  starting transfers between devices: 35.9 us -> 37.7 us
    ppermute x21, waiting for transfers between devices: 45.6 us -> 43.7 us  [hop(): return lax.ppermute(value, axis, [(i, i ^ mask) for i in range(size)])]
    ppermute x21, starting transfers between devices: 27.9 us -> 29.6 us  [hop(): return lax.ppermute(value, axis, [(i, i ^ mask) for i in range(size)])]
where the time goes in v1:
time: 99.9 us; the launch traced here: 99.6 us
  waiting for transfers between devices  51.7 us (52%)
  starting transfers between devices  37.7 us (38%)
  Pallas kernels  6.39 us (6%)
  other arithmetic  1.75 us (2%)
  local copies, waits for them, and re-layouts  1.2 us (1%)
    ppermute x21, waiting for transfers between devices, hop(): return lax.ppermute(value, axis, [(i, i ^ mask) for i in range(size)])  43.7 us
    ppermute x21, starting transfers between devices, hop(): return lax.ppermute(value, axis, [(i, i ^ mask) for i in range(size)])  29.6 us
    all_to_all x1, starting transfers between devices, per_device(): lax.all_to_all(after(turned, held), 'tile', split_axis=0, concat_axis=0,...  8.04 us
    all_to_all x1, waiting for transfers between devices, per_device(): lax.all_to_all(after(turned, held), 'tile', split_axis=0, concat_axis=0,...  8.02 us
    pallas_call x6, Pallas kernels, call(): pl.pallas_call(kernel, out_shape=[jax.ShapeDtypeStruct(s, d) for s, d in...  6.39 us
  transfers between devices with their start and end apart: 22, of which 16 were waited for; matrix products, arithmetic and copies ran while one was open for 1% of the time, Pallas kernels for 2%

profile of v1, /device:TPU:32, one launch (start us, length us, event | category | flops | bytes accessed | tf_op | source)
XLA Modules:
  0.0 99.6 jit_solution(9965289914847430425)
XLA Ops:
  0.6 0.0 copy-start.4
  0.6 0.0 copy-start.5
  0.7 0.8 pad_maximum_fusion.1
  1.5 3.4 %collective-permute-start.1 = (bf16[1,32,1024]{2,1,0:T(8,128)(2,1)S(1)}, bf16[1,32,1024]{2,1,0:T(8,128)(2,1)S(1)}, u32[]{:S(2)}, u32[]{:S(2)}) collective-permute-start(bf16[1,32,1024]{2,1,0:T(8,128)(2,1)S(1)} %get-tuple-element.39), channel_id=1, source_target_pairs={{0,128},{8,136},{16,144},{24,152},{32,160},{40,168},{48,176},{56,1... | collective-permute-start | bytes 196616 | tf_op jit(solution)/shard_map/ppermute | solution.py:24
  4.8 0.1 collective-permute-start
  5.0 0.6 collective-permute-start.2
  5.5 0.0 copy-start
  5.5 1.1 %copy-done = bf16[9,32,1024]{2,1,0:T(8,128)(2,1)S(1)} copy-done((bf16[9,32,1024]{2,1,0:T(8,128)(2,1)S(1)}, bf16[9,32,1024]{2,1,0:T(8,128)(2,1)}, u32[]{:S(2)}) %copy-start) | copy-done | bytes 589848
  6.6 1.2 %shard_map.101 = bf16[32,72,128]{2,1,0:T(8,128)(2,1)} custom-call(bf16[288,1024]{1,0:T(8,128)(2,1)S(1)} %bitcast.36), custom_call_target="tpu_custom_call" | custom-call | bytes 4194304 | tf_op jit(solution)/shard_map/pallas_call | solution.py:174
  7.8 0.4 collective-permute-done.1
  8.1 1.1 %collective-permute-done = bf16[1,32,1024]{2,1,0:T(8,128)(2,1)S(1)} collective-permute-done((bf16[1,32,1024]{2,1,0:T(8,128)(2,1)S(1)}, bf16[1,32,1024]{2,1,0:T(8,128)(2,1)S(1)}, u32[]{:S(2)}, u32[]{:S(2)}) %collective-permute-start) | collective-permute-done | bytes 65568 | tf_op jit(solution)/shard_map/ppermute | solution.py:24
  9.3 0.7 collective-permute-done.2
  10.0 0.0 copy-done.4
  10.0 0.0 copy-done.5
  10.0 3.1 %collective-permute-start.5 = (bf16[4,32,1024]{2,1,0:T(8,128)(2,1)S(1)}, bf16[4,32,1024]{2,1,0:T(8,128)(2,1)S(1)}, u32[]{:S(2)}, u32[]{:S(2)}) collective-permute-start(bf16[4,32,1024]{2,1,0:T(8,128)(2,1)S(1)} %pad_maximum_fusion), channel_id=1, source_target_pairs={{0,48},{8,56},{16,32},{24,40},{32,16},{40,24},{48,0},{56,8},{64,11... | collective-permute-start | bytes 786440 | tf_op jit(solution)/shard_map/ppermute | solution.py:24
  13.1 0.6 collective-permute-start.4
  13.7 0.5 collective-permute-start.3
  14.2 8.0 %all-to-all-start = ((bf16[32,72,128]{2,1,0:T(8,128)(2,1)}), bf16[32,72,128]{2,1,0:T(8,128)(2,1)S(1)}, u32[]{:S(2)}, u32[]{:S(2)}) async-start(bf16[32,72,128]{2,1,0:T(8,128)(2,1)} %shard_map.101), calls=%async_computation | async-start | bytes 1179648 | tf_op jit(solution)/shard_map/all_to_all | solution.py:229
  22.2 0.0 copy-start.1
  22.3 4.7 %collective-permute-done.3 = bf16[4,32,1024]{2,1,0:T(8,128)(2,1)S(1)} collective-permute-done((bf16[4,32,1024]{2,1,0:T(8,128)(2,1)S(1)}, bf16[4,32,1024]{2,1,0:T(8,128)(2,1)S(1)}, u32[]{:S(2)}, u32[]{:S(2)}) %collective-permute-start.3) | collective-permute-done | bytes 262176 | tf_op jit(solution)/shard_map/ppermute | solution.py:24
  27.0 0.0 collective-permute-done.4
  27.0 0.0 collective-permute-done.5
  27.1 0.1 collective-permute-start.6
  27.2 2.6 %collective-permute-done.6.far_ref = bf16[16,32,1024]{2,1,0:T(8,128)(2,1)S(1)} collective-permute-done((bf16[16,32,1024]{2,1,0:T(8,128)(2,1)S(1)}, bf16[16,32,1024]{2,1,0:T(8,128)(2,1)S(1)}, u32[]{:S(2)}, u32[]{:S(2)}) %collective-permute-start.6) | collective-permute-done | bytes 1048608 | tf_op jit(solution)/shard_map/ppermute | solution.py:24
  29.8 0.0 copy-done.1
  29.8 1.0 shard_map.102.state_ref
  30.8 8.0 %all-to-all-done.w2_ref = bf16[32,72,128]{2,1,0:T(8,128)(2,1)S(1)} async-done(((bf16[32,72,128]{2,1,0:T(8,128)(2,1)}), bf16[32,72,128]{2,1,0:T(8,128)(2,1)S(1)}, u32[]{:S(2)}, u32[]{:S(2)}) %all-to-all-start) | async-done | bytes 589856 | tf_op jit(solution)/shard_map/all_to_all | solution.py:229
  38.8 0.0 copy-done.2
  38.8 0.0 copy-done.3
  38.8 2.5 %shard_map.103 = (f32[256,1024]{1,0:T(8,128)S(1)}, f32[256,1024]{1,0:T(8,128)S(1)}, f32[592,256]{1,0:T(8,128)S(1)}, bf16[592,256]{1,0:T(8,128)(2,1)S(1)}, bf16[5...) custom-call(bf16[16,32,1024]{2,1,0:T(8,128)(2,1)S(1)} %constant_dynamic-update-slice_fusion.near_ref, ...), custom_call_target="tpu_custom_call" | custom-call | flops 1207959552 | bytes 4194304 | tf_op jit(solution)/shard_map/pallas_call | solution.py:174
  41.3 0.7 collective-permute-start.7
  42.0 1.5 %collective-permute-start.11 = (bf16[592,256]{1,0:T(8,128)(2,1)S(1)}, bf16[592,256]{1,0:T(8,128)(2,1)S(1)}, u32[]{:S(2)}, u32[]{:S(2)}) collective-permute-start(bf16[592,256]{1,0:T(8,128)(2,1)S(1)} %get-tuple-element.22), channel_id=1, source_target_pairs={{0,2},{1,3},{2,0},{3,1},{4,6},{5,7},{6,4},{7,5},{8,10},{9,11},{10,... | collective-permute-start | bytes 909320 | tf_op jit(solution)/shard_map/ppermute | solution.py:24
  43.5 2.7 %collective-permute-start.12 = (bf16[592,256]{1,0:T(8,128)(2,1)S(1)}, bf16[592,256]{1,0:T(8,128)(2,1)S(1)}, u32[]{:S(2)}, u32[]{:S(2)}) collective-permute-start(bf16[592,256]{1,0:T(8,128)(2,1)S(1)} %get-tuple-element.23), channel_id=1, source_target_pairs={{0,4},{1,5},{2,6},{3,7},{4,0},{5,1},{6,2},{7,3},{8,12},{9,13},{10,... | collective-permute-start | bytes 909320 | tf_op jit(solution)/shard_map/ppermute | solution.py:24
  46.2 0.5 collective-permute-start.13
  46.7 5.3 %collective-permute-done.11.r1 = bf16[592,256]{1,0:T(8,128)(2,1)S(1)} collective-permute-done((bf16[592,256]{1,0:T(8,128)(2,1)S(1)}, bf16[592,256]{1,0:T(8,128)(2,1)S(1)}, u32[]{:S(2)}, u32[]{:S(2)}) %collective-permute-start.11) | collective-permute-done | bytes 303136 | tf_op jit(solution)/shard_map/ppermute | solution.py:24
  52.0 8.0 %collective-permute-done.12.r2 = bf16[592,256]{1,0:T(8,128)(2,1)S(1)} collective-permute-done((bf16[592,256]{1,0:T(8,128)(2,1)S(1)}, bf16[592,256]{1,0:T(8,128)(2,1)S(1)}, u32[]{:S(2)}, u32[]{:S(2)}) %collective-permute-start.12) | collective-permute-done | bytes 303136 | tf_op jit(solution)/shard_map/ppermute | solution.py:24
  60.0 2.6 %collective-permute-done.13.r3 = bf16[592,256]{1,0:T(8,128)(2,1)S(1)} collective-permute-done((bf16[592,256]{1,0:T(8,128)(2,1)S(1)}, bf16[592,256]{1,0:T(8,128)(2,1)S(1)}, u32[]{:S(2)}, u32[]{:S(2)}) %collective-permute-start.13) | collective-permute-done | bytes 303136 | tf_op jit(solution)/shard_map/ppermute | solution.py:24
  62.6 0.1 shard_map.104.mine_ref
  62.7 5.6 %collective-permute-start.14 = (bf16[592,256]{1,0:T(8,128)(2,1)S(1)}, bf16[592,256]{1,0:T(8,128)(2,1)S(1)}, u32[]{:S(2)}, u32[]{:S(2)}) collective-permute-start(bf16[592,256]{1,0:T(8,128)(2,1)S(1)} %shard_map.104.mine_ref), channel_id=1, source_target_pairs={{0,1},{1,0},{2,3},{3,2},{4,5},{5,4},{6,7},{7,6},{8,9},{9,8},{10,11... | collective-permute-start | bytes 909320 | tf_op jit(solution)/shard_map/ppermute | solution.py:24
  68.3 0.0 collective-permute-done.7
  68.3 0.2 fusion.7
  68.5 0.7 collective-permute-start.8
  69.2 1.1 %collective-permute-start.10 = (bf16[64,1024]{1,0:T(8,128)(2,1)S(1)}, bf16[64,1024]{1,0:T(8,128)(2,1)S(1)}, u32[]{:S(2)}, u32[]{:S(2)}) collective-permute-start(bf16[64,1024]{1,0:T(8,128)(2,1)S(1)} %get-tuple-element.34), channel_id=1, source_target_pairs={{0,48},{8,56},{16,32},{24,40},{32,16},{40,24},{48,0},{56,8},{64,11... | collective-permute-start | bytes 393224 | tf_op jit(solution)/shard_map/ppermute | solution.py:24
  70.3 2.4 %collective-permute-start.9 = (bf16[64,1024]{1,0:T(8,128)(2,1)S(1)}, bf16[64,1024]{1,0:T(8,128)(2,1)S(1)}, u32[]{:S(2)}, u32[]{:S(2)}) collective-permute-start(bf16[64,1024]{1,0:T(8,128)(2,1)S(1)} %get-tuple-element.35), channel_id=1, source_target_pairs={{0,32},{8,40},{16,48},{24,56},{32,0},{40,8},{48,16},{56,24},{64,96... | collective-permute-start | bytes 393224 | tf_op jit(solution)/shard_map/ppermute | solution.py:24
  72.7 1.7 %collective-permute-done.8 = bf16[64,1024]{1,0:T(8,128)(2,1)S(1)} collective-permute-done((bf16[64,1024]{1,0:T(8,128)(2,1)S(1)}, bf16[64,1024]{1,0:T(8,128)(2,1)S(1)}, u32[]{:S(2)}, u32[]{:S(2)}) %collective-permute-start.8) | collective-permute-done | bytes 131104 | tf_op jit(solution)/shard_map/ppermute | solution.py:24
  74.4 3.0 %collective-permute-done.10 = bf16[64,1024]{1,0:T(8,128)(2,1)S(1)} collective-permute-done((bf16[64,1024]{1,0:T(8,128)(2,1)S(1)}, bf16[64,1024]{1,0:T(8,128)(2,1)S(1)}, u32[]{:S(2)}, u32[]{:S(2)}) %collective-permute-start.10) | collective-permute-done | bytes 131104 | tf_op jit(solution)/shard_map/ppermute | solution.py:24
  77.4 0.0 collective-permute-done.9
  77.4 3.6 %collective-permute-done.14.other_ref = bf16[592,256]{1,0:T(8,128)(2,1)S(1)} collective-permute-done((bf16[592,256]{1,0:T(8,128)(2,1)S(1)}, bf16[592,256]{1,0:T(8,128)(2,1)S(1)}, u32[]{:S(2)}, u32[]{:S(2)}) %collective-permute-start.14) | collective-permute-done | bytes 303136 | tf_op jit(solution)/shard_map/ppermute | solution.py:24
  81.0 0.1 shard_map.105.a0
  81.1 0.6 collective-permute-start.20
  81.7 0.0 collective-permute-start.19
  81.7 3.6 %collective-permute-start.18 = (bf16[592,256]{1,0:T(8,128)(2,1)S(1)}, bf16[592,256]{1,0:T(8,128)(2,1)S(1)}, u32[]{:S(2)}, u32[]{:S(2)}) collective-permute-start(bf16[592,256]{1,0:T(8,128)(2,1)S(1)} %shard_map.105.a0), channel_id=1, source_target_pairs={{0,2},{1,3},{2,0},{3,1},{4,6},{5,7},{6,4},{7,5},{8,10},{9,11},{10,... | collective-permute-start | bytes 909320 | tf_op jit(solution)/shard_map/ppermute | solution.py:24
  85.3 0.1 fusion.1
  85.4 0.1 collective-permute-start.15
  85.5 1.3 %collective-permute-start.17 = (bf16[16,1024]{1,0:T(8,128)(2,1)S(1)}, bf16[16,1024]{1,0:T(8,128)(2,1)S(1)}, u32[]{:S(2)}, u32[]{:S(2)}) collective-permute-start(bf16[16,1024]{1,0:T(8,128)(2,1)S(1)} %get-tuple-element.37), channel_id=1, source_target_pairs={{0,192},{8,200},{16,208},{24,216},{32,224},{40,232},{48,240},{56,2... | collective-permute-start | bytes 98312 | tf_op jit(solution)/shard_map/ppermute | solution.py:24
  86.8 2.6 %collective-permute-done.15 = bf16[16,1024]{1,0:T(8,128)(2,1)S(1)} collective-permute-done((bf16[16,1024]{1,0:T(8,128)(2,1)S(1)}, bf16[16,1024]{1,0:T(8,128)(2,1)S(1)}, u32[]{:S(2)}, u32[]{:S(2)}) %collective-permute-start.15) | collective-permute-done | bytes 32800 | tf_op jit(solution)/shard_map/ppermute | solution.py:24
  89.4 0.6 collective-permute-start.16
  90.0 0.0 collective-permute-done.17
  90.0 4.2 %collective-permute-done.16 = bf16[16,1024]{1,0:T(8,128)(2,1)S(1)} collective-permute-done((bf16[16,1024]{1,0:T(8,128)(2,1)S(1)}, bf16[16,1024]{1,0:T(8,128)(2,1)S(1)}, u32[]{:S(2)}, u32[]{:S(2)}) %collective-permute-start.16) | collective-permute-done | bytes 32800 | tf_op jit(solution)/shard_map/ppermute | solution.py:24
  94.2 0.6 fusion.6
  94.9 2.5 %collective-permute-done.20.a3 = bf16[592,256]{1,0:T(8,128)(2,1)S(1)} collective-permute-done((bf16[592,256]{1,0:T(8,128)(2,1)S(1)}, bf16[592,256]{1,0:T(8,128)(2,1)S(1)}, u32[]{:S(2)}, u32[]{:S(2)}) %collective-permute-start.20) | collective-permute-done | bytes 303136 | tf_op jit(solution)/shard_map/ppermute | solution.py:24
  97.4 0.0 collective-permute-done.19.a2
  97.4 0.6 collective-permute-done.18.a1
  98.0 1.6 %shard_map.106 = (f32[288,1024]{1,0:T(8,128)}, f32[288,1024]{1,0:T(8,128)}, f32[1,32]{1,0:T(1,128)}, f32[1,32]{1,0:T(1,128)}) custom-call(bf16[592,256]{1,0:T(8,128)(2,1)S(1)} %shard_map.105.a0, bf16[592,256]{1,0:T(8,128)(2,1)S(1)} %collective-permute-done.18.a1, bf16[592,256]{1,0:T(8,128)(2,1)S(1)} %collective-permute-done.19.a2, ...), custom_call_target="tpu_custom_call" | custom-call | bytes 4194304 | tf_op jit(solution)/shard_map/pallas_call | solution.py:174
  (12 shorter events, 0.2 us)
Async XLA Ops:
  0.6 9.3 %copy-start.4 = (bf16[1,16,1,1024]{3,1,2,0:T(8,128)(2,1)S(1)}, bf16[1,16,1,1024]{3,1,2,0:T(8,128)(2,1)}, u32[]{:S(2)}) copy-start(bf16[1,16,1,1024]{3,1,2,0:T(8,128)(2,1)} %param.11) | copy-start | bytes 98308
  0.6 9.3 %copy-start.5 = (bf16[1,16,1,1024]{3,1,2,0:T(8,128)(2,1)S(1)}, bf16[1,16,1,1024]{3,1,2,0:T(8,128)(2,1)}, u32[]{:S(2)}) copy-start(bf16[1,16,1,1024]{3,1,2,0:T(8,128)(2,1)} %param.6) | copy-start | bytes 98308
  1.5 6.7 %collective-permute-start.1 = (bf16[1,32,1024]{2,1,0:T(8,128)(2,1)S(1)}, bf16[1,32,1024]{2,1,0:T(8,128)(2,1)S(1)}, u32[]{:S(2)}, u32[]{:S(2)}) collective-permute-start(bf16[1,32,1024]{2,1,0:T(8,128)(2,1)S(1)} %get-tuple-element.39), channel_id=1, source_target_pairs={{0,128},{8,136},{16,144},{24,152},{32,160},{40,168},{48,176},{56,1... | collective-permute-start | bytes 196616 | tf_op jit(solution)/shard_map/ppermute | solution.py:24
  4.8 4.5 %collective-permute-start = (bf16[1,32,1024]{2,1,0:T(8,128)(2,1)S(1)}, bf16[1,32,1024]{2,1,0:T(8,128)(2,1)S(1)}, u32[]{:S(2)}, u32[]{:S(2)}) collective-permute-start(bf16[1,32,1024]{2,1,0:T(8,128)(2,1)S(1)} %get-tuple-element.39), channel_id=1, source_target_pairs={{0,64},{8,72},{16,80},{24,88},{32,96},{40,104},{48,112},{56,120},{... | collective-permute-start | bytes 196616 | tf_op jit(solution)/shard_map/ppermute | solution.py:24
  5.0 5.0 %collective-permute-start.2 = (bf16[1,32,1024]{2,1,0:T(8,128)(2,1)S(1)}, bf16[1,32,1024]{2,1,0:T(8,128)(2,1)S(1)}, u32[]{:S(2)}, u32[]{:S(2)}) collective-permute-start(bf16[1,32,1024]{2,1,0:T(8,128)(2,1)S(1)} %get-tuple-element.39), channel_id=1, source_target_pairs={{0,192},{8,200},{16,208},{24,216},{32,224},{40,232},{48,240},{56,2... | collective-permute-start | bytes 196616 | tf_op jit(solution)/shard_map/ppermute | solution.py:24
  5.5 1.1 %copy-start = (bf16[9,32,1024]{2,1,0:T(8,128)(2,1)S(1)}, bf16[9,32,1024]{2,1,0:T(8,128)(2,1)}, u32[]{:S(2)}) copy-start(bf16[9,32,1024]{2,1,0:T(8,128)(2,1)} %param.8) | copy-start | bytes 1769476
  10.0 17.1 %collective-permute-start.5 = (bf16[4,32,1024]{2,1,0:T(8,128)(2,1)S(1)}, bf16[4,32,1024]{2,1,0:T(8,128)(2,1)S(1)}, u32[]{:S(2)}, u32[]{:S(2)}) collective-permute-start(bf16[4,32,1024]{2,1,0:T(8,128)(2,1)S(1)} %pad_maximum_fusion), channel_id=1, source_target_pairs={{0,48},{8,56},{16,32},{24,40},{32,16},{40,24},{48,0},{56,8},{64,11... | collective-permute-start | bytes 786440 | tf_op jit(solution)/shard_map/ppermute | solution.py:24
  13.1 13.9 %collective-permute-start.4 = (bf16[4,32,1024]{2,1,0:T(8,128)(2,1)S(1)}, bf16[4,32,1024]{2,1,0:T(8,128)(2,1)S(1)}, u32[]{:S(2)}, u32[]{:S(2)}) collective-permute-start(bf16[4,32,1024]{2,1,0:T(8,128)(2,1)S(1)} %pad_maximum_fusion), channel_id=1, source_target_pairs={{0,32},{8,40},{16,48},{24,56},{32,0},{40,8},{48,16},{56,24},{64,96... | collective-permute-start | bytes 786440 | tf_op jit(solution)/shard_map/ppermute | solution.py:24
  13.7 13.3 %collective-permute-start.3 = (bf16[4,32,1024]{2,1,0:T(8,128)(2,1)S(1)}, bf16[4,32,1024]{2,1,0:T(8,128)(2,1)S(1)}, u32[]{:S(2)}, u32[]{:S(2)}) collective-permute-start(bf16[4,32,1024]{2,1,0:T(8,128)(2,1)S(1)} %pad_maximum_fusion), channel_id=1, source_target_pairs={{0,16},{8,24},{16,0},{24,8},{32,48},{40,56},{48,32},{56,40},{64,80... | collective-permute-start | bytes 786440 | tf_op jit(solution)/shard_map/ppermute | solution.py:24
  14.2 24.7 %all-to-all-start = ((bf16[32,72,128]{2,1,0:T(8,128)(2,1)}), bf16[32,72,128]{2,1,0:T(8,128)(2,1)S(1)}, u32[]{:S(2)}, u32[]{:S(2)}) async-start(bf16[32,72,128]{2,1,0:T(8,128)(2,1)} %shard_map.101), calls=%async_computation | async-start | bytes 1179648 | tf_op jit(solution)/shard_map/all_to_all | solution.py:229
  22.2 7.6 %copy-start.1 = (bf16[9,32,1024]{2,1,0:T(8,128)(2,1)S(1)}, bf16[9,32,1024]{2,1,0:T(8,128)(2,1)}, u32[]{:S(2)}) copy-start(bf16[9,32,1024]{2,1,0:T(8,128)(2,1)} %param.7) | copy-start | bytes 1769476
  27.1 2.7 %collective-permute-start.6 = (bf16[16,32,1024]{2,1,0:T(8,128)(2,1)S(1)}, bf16[16,32,1024]{2,1,0:T(8,128)(2,1)S(1)}, u32[]{:S(2)}, u32[]{:S(2)}) collective-permute-start(bf16[16,32,1024]{2,1,0:T(8,128)(2,1)S(1)} %constant_dynamic-update-slice_fusion.near_ref), channel_id=1, source_target_pairs={{0,8},{8,0},{16,24},{24,16},{32,40},{40,32},{48,56},{56,48},{64,72... | collective-permute-start | bytes 3145736 | tf_op jit(solution)/shard_map/ppermute | solution.py:24
  29.8 9.0 %copy-start.2 = (f32[32]{0:T(128)S(1)}, f32[32]{0:T(128)}, u32[]{:S(2)}) copy-start(f32[32]{0:T(128)} %param.9) | copy-start | bytes 388
  29.8 9.0 %copy-start.3 = (f32[32]{0:T(128)S(1)}, f32[32]{0:T(128)}, u32[]{:S(2)}) copy-start(f32[32]{0:T(128)} %param.10) | copy-start | bytes 388
  41.3 27.0 %collective-permute-start.7 = (f32[256,1024]{1,0:T(8,128)S(1)}, f32[256,1024]{1,0:T(8,128)S(1)}, u32[]{:S(2)}, u32[]{:S(2)}) collective-permute-start(f32[256,1024]{1,0:T(8,128)S(1)} %get-tuple-element.20), channel_id=1, source_target_pairs={{0,8},{8,0},{16,24},{24,16},{32,40},{40,32},{48,56},{56,48},{64,72... | collective-permute-start | bytes 3145736 | tf_op jit(solution)/shard_map/ppermute | solution.py:24
  42.0 10.0 %collective-permute-start.11 = (bf16[592,256]{1,0:T(8,128)(2,1)S(1)}, bf16[592,256]{1,0:T(8,128)(2,1)S(1)}, u32[]{:S(2)}, u32[]{:S(2)}) collective-permute-start(bf16[592,256]{1,0:T(8,128)(2,1)S(1)} %get-tuple-element.22), channel_id=1, source_target_pairs={{0,2},{1,3},{2,0},{3,1},{4,6},{5,7},{6,4},{7,5},{8,10},{9,11},{10,... | collective-permute-start | bytes 909320 | tf_op jit(solution)/shard_map/ppermute | solution.py:24
  43.5 16.5 %collective-permute-start.12 = (bf16[592,256]{1,0:T(8,128)(2,1)S(1)}, bf16[592,256]{1,0:T(8,128)(2,1)S(1)}, u32[]{:S(2)}, u32[]{:S(2)}) collective-permute-start(bf16[592,256]{1,0:T(8,128)(2,1)S(1)} %get-tuple-element.23), channel_id=1, source_target_pairs={{0,4},{1,5},{2,6},{3,7},{4,0},{5,1},{6,2},{7,3},{8,12},{9,13},{10,... | collective-permute-start | bytes 909320 | tf_op jit(solution)/shard_map/ppermute | solution.py:24
  46.2 16.3 %collective-permute-start.13 = (bf16[592,256]{1,0:T(8,128)(2,1)S(1)}, bf16[592,256]{1,0:T(8,128)(2,1)S(1)}, u32[]{:S(2)}, u32[]{:S(2)}) collective-permute-start(bf16[592,256]{1,0:T(8,128)(2,1)S(1)} %get-tuple-element.24), channel_id=1, source_target_pairs={{0,6},{1,7},{2,4},{3,5},{4,2},{5,3},{6,0},{7,1},{8,14},{9,15},{10,... | collective-permute-start | bytes 909320 | tf_op jit(solution)/shard_map/ppermute | solution.py:24
  62.7 18.3 %collective-permute-start.14 = (bf16[592,256]{1,0:T(8,128)(2,1)S(1)}, bf16[592,256]{1,0:T(8,128)(2,1)S(1)}, u32[]{:S(2)}, u32[]{:S(2)}) collective-permute-start(bf16[592,256]{1,0:T(8,128)(2,1)S(1)} %shard_map.104.mine_ref), channel_id=1, source_target_pairs={{0,1},{1,0},{2,3},{3,2},{4,5},{5,4},{6,7},{7,6},{8,9},{9,8},{10,11... | collective-permute-start | bytes 909320 | tf_op jit(solution)/shard_map/ppermute | solution.py:24
  68.5 5.9 %collective-permute-start.8 = (bf16[64,1024]{1,0:T(8,128)(2,1)S(1)}, bf16[64,1024]{1,0:T(8,128)(2,1)S(1)}, u32[]{:S(2)}, u32[]{:S(2)}) collective-permute-start(bf16[64,1024]{1,0:T(8,128)(2,1)S(1)} %get-tuple-element.33), channel_id=1, source_target_pairs={{0,16},{8,24},{16,0},{24,8},{32,48},{40,56},{48,32},{56,40},{64,80... | collective-permute-start | bytes 393224 | tf_op jit(solution)/shard_map/ppermute | solution.py:24
  69.2 8.3 %collective-permute-start.10 = (bf16[64,1024]{1,0:T(8,128)(2,1)S(1)}, bf16[64,1024]{1,0:T(8,128)(2,1)S(1)}, u32[]{:S(2)}, u32[]{:S(2)}) collective-permute-start(bf16[64,1024]{1,0:T(8,128)(2,1)S(1)} %get-tuple-element.34), channel_id=1, source_target_pairs={{0,48},{8,56},{16,32},{24,40},{32,16},{40,24},{48,0},{56,8},{64,11... | collective-permute-start | bytes 393224 | tf_op jit(solution)/shard_map/ppermute | solution.py:24
  70.3 7.2 %collective-permute-start.9 = (bf16[64,1024]{1,0:T(8,128)(2,1)S(1)}, bf16[64,1024]{1,0:T(8,128)(2,1)S(1)}, u32[]{:S(2)}, u32[]{:S(2)}) collective-permute-start(bf16[64,1024]{1,0:T(8,128)(2,1)S(1)} %get-tuple-element.35), channel_id=1, source_target_pairs={{0,32},{8,40},{16,48},{24,56},{32,0},{40,8},{48,16},{56,24},{64,96... | collective-permute-start | bytes 393224 | tf_op jit(solution)/shard_map/ppermute | solution.py:24
  81.1 16.3 %collective-permute-start.20 = (bf16[592,256]{1,0:T(8,128)(2,1)S(1)}, bf16[592,256]{1,0:T(8,128)(2,1)S(1)}, u32[]{:S(2)}, u32[]{:S(2)}) collective-permute-start(bf16[592,256]{1,0:T(8,128)(2,1)S(1)} %shard_map.105.a0), channel_id=1, source_target_pairs={{0,6},{1,7},{2,4},{3,5},{4,2},{5,3},{6,0},{7,1},{8,14},{9,15},{10,... | collective-permute-start | bytes 909320 | tf_op jit(solution)/shard_map/ppermute | solution.py:24
  81.7 15.7 %collective-permute-start.19 = (bf16[592,256]{1,0:T(8,128)(2,1)S(1)}, bf16[592,256]{1,0:T(8,128)(2,1)S(1)}, u32[]{:S(2)}, u32[]{:S(2)}) collective-permute-start(bf16[592,256]{1,0:T(8,128)(2,1)S(1)} %shard_map.105.a0), channel_id=1, source_target_pairs={{0,4},{1,5},{2,6},{3,7},{4,0},{5,1},{6,2},{7,3},{8,12},{9,13},{10,... | collective-permute-start | bytes 909320 | tf_op jit(solution)/shard_map/ppermute | solution.py:24
  81.7 16.3 %collective-permute-start.18 = (bf16[592,256]{1,0:T(8,128)(2,1)S(1)}, bf16[592,256]{1,0:T(8,128)(2,1)S(1)}, u32[]{:S(2)}, u32[]{:S(2)}) collective-permute-start(bf16[592,256]{1,0:T(8,128)(2,1)S(1)} %shard_map.105.a0), channel_id=1, source_target_pairs={{0,2},{1,3},{2,0},{3,1},{4,6},{5,7},{6,4},{7,5},{8,10},{9,11},{10,... | collective-permute-start | bytes 909320 | tf_op jit(solution)/shard_map/ppermute | solution.py:24
  85.4 4.0 %collective-permute-start.15 = (bf16[16,1024]{1,0:T(8,128)(2,1)S(1)}, bf16[16,1024]{1,0:T(8,128)(2,1)S(1)}, u32[]{:S(2)}, u32[]{:S(2)}) collective-permute-start(bf16[16,1024]{1,0:T(8,128)(2,1)S(1)} %get-tuple-element.36), channel_id=1, source_target_pairs={{0,64},{8,72},{16,80},{24,88},{32,96},{40,104},{48,112},{56,120},{... | collective-permute-start | bytes 98312 | tf_op jit(solution)/shard_map/ppermute | solution.py:24
  85.5 4.5 %collective-permute-start.17 = (bf16[16,1024]{1,0:T(8,128)(2,1)S(1)}, bf16[16,1024]{1,0:T(8,128)(2,1)S(1)}, u32[]{:S(2)}, u32[]{:S(2)}) collective-permute-start(bf16[16,1024]{1,0:T(8,128)(2,1)S(1)} %get-tuple-element.37), channel_id=1, source_target_pairs={{0,192},{8,200},{16,208},{24,216},{32,224},{40,232},{48,240},{56,2... | collective-permute-start | bytes 98312 | tf_op jit(solution)/shard_map/ppermute | solution.py:24
  89.4 4.8 %collective-permute-start.16 = (bf16[16,1024]{1,0:T(8,128)(2,1)S(1)}, bf16[16,1024]{1,0:T(8,128)(2,1)S(1)}, u32[]{:S(2)}, u32[]{:S(2)}) collective-permute-start(bf16[16,1024]{1,0:T(8,128)(2,1)S(1)} %get-tuple-element.38), channel_id=1, source_target_pairs={{0,128},{8,136},{16,144},{24,152},{32,160},{40,168},{48,176},{56,1... | collective-permute-start | bytes 98312 | tf_op jit(solution)/shard_map/ppermute | solution.py:24
